TPU v7x, 256 devices: a whole 4x4x8 slice. The times are simulated.
256 devices in a mesh: box: 64 (over z, y, core), col: 4 (over x).
Axes of the slice: x: 4, y: 4, z: 8, core: 2. Of those that a mesh axis runs over, the one named last changes fastest.
Arguments:
- box_points: float32 [128, 3, 512], P('box'), may hold values from 0 to 1
- proxy_directions: float32 [3, 1024], P(None, 'col'), may hold values from -1 to 1, as said below
- point_order: int32 [128, 512], P('box'), may hold values from 0 to 511, each once within a row
- neighbour_boxes: int32 [128, 8], P('box'), may hold values from 0 to 127, as said below
- neighbour_places: int32 [128, 8], P('box'), may hold values from 0 to 25
- pivot_inverse: float32 [128, 2, 256], P('box', None, 'col'), may hold values from -6 to 6
Outputs:
- interpolation: float32 [128, 2, 256, 256], P('box', None, None, 'col')
- skeleton_update: float32 [128, 2, 256, 256], P('box', None, 'col')
Inputs may be any that keep to these rules, and one draw needn't show every extreme that they name: `neighbour_boxes`: box g is held by index g // 2 of the box axis. Every entry names a box of the same index or of the index just before or just after it, cyclically. Of the 16 entries of one index's boxes exactly half name boxes of that same index, never the listing box itself; a box may be listed twice in one row. `proxy_directions`: unit vectors.
All inputs are finite; a program needn't handle non-finite values.
Results may differ from a plain program's by a relative error of at most 0.0038.
Values sent between devices are 32-bit elements; how exact they have to be, the bound alone decides.
No kernel may reach another device: no remote copies, remote signals or barrier semaphores. Data moves between devices by JAX's collectives and lax.ppermute only.
A program may use at most 64 MiB of HBM per device.

v0:
```python
import math

import jax
import jax.numpy as jnp
from jax import lax
from jax.sharding import PartitionSpec as P

S = 256


wavenumber = 4.0 * math.pi
softening = 0.05
proxy_radius = 1.5
ridge_share = 0.05
highest = lax.Precision.HIGHEST


def padded(block, sides, width):
    for axis, dim in sides:
        count = lax.axis_size(axis)
        forward = [(i, i + 1) for i in range(count - 1)]
        forward.append((count - 1, 0))
        backward = [(target, source) for source, target in forward]
        low = lax.ppermute(
            lax.slice_in_dim(block, block.shape[dim] - width, None, axis=dim), axis, forward
        )
        high = lax.ppermute(lax.slice_in_dim(block, 0, width, axis=dim), axis, backward)
        block = jnp.concatenate([low, block, high], axis=dim)
    return block


def helmholtz(targets, sources):
    distance_sq = jnp.zeros((targets.shape[1], sources.shape[1]), targets.dtype)
    for axis_id in range(3):
        difference = targets[axis_id][:, None] - sources[axis_id][None, :]
        distance_sq = distance_sq + difference * difference
    radius = jnp.sqrt(distance_sq + softening * softening)
    amplitude = 1.0 / (4.0 * math.pi * radius)
    return (amplitude * jnp.cos(wavenumber * radius), amplitude * jnp.sin(wavenumber * radius))


def decode(place_codes):
    full_code = place_codes + (place_codes >= 13).astype(jnp.int32)
    return jnp.stack(
        [full_code // 9 - 1, full_code // 3 % 3 - 1, full_code % 3 - 1], axis=-1
    ).astype(jnp.float32)


def cross_products(real_tile, imag_tile, skel_count):
    stacked = jnp.concatenate([real_tile, imag_tile], axis=0)
    flipped = jnp.concatenate([imag_tile, -real_tile], axis=0)
    left_cols = stacked[:, :skel_count]
    contract = (((0,), (0,)), ((), ()))
    real_cross = lax.dot_general(left_cols, stacked, contract, preferred_element_type=jnp.float32)
    imag_cross = lax.dot_general(left_cols, flipped, contract, preferred_element_type=jnp.float32)
    return jnp.stack([real_cross, imag_cross])


def factor(gram_block):
    real_gram = gram_block[0]
    imag_gram = gram_block[1]
    skel_count = real_gram.shape[0]
    ridge_value = ridge_share * jnp.trace(real_gram) / skel_count
    real_gram = real_gram + ridge_value * jnp.eye(skel_count, dtype=real_gram.dtype)
    upper_half = jnp.concatenate([real_gram, -imag_gram], axis=1)
    lower_half = jnp.concatenate([imag_gram, real_gram], axis=1)
    return jnp.linalg.cholesky(jnp.concatenate([upper_half, lower_half], axis=0))


def apply_inverse(cholesky_factor, right_side):
    stacked = right_side.reshape(2 * right_side.shape[1], right_side.shape[2])
    forward = lax.linalg.triangular_solve(cholesky_factor, stacked, left_side=True, lower=True)
    backward = lax.linalg.triangular_solve(
        cholesky_factor, forward, left_side=True, lower=True, transpose_a=True
    )
    return backward.reshape(right_side.shape)


def pair_update(near_points, own_columns, coefficients, pivot_row):
    skel_count = coefficients.shape[1]
    real_kernel, imag_kernel = helmholtz(near_points, own_columns)
    real_skel = real_kernel[:, :skel_count]
    imag_skel = imag_kernel[:, :skel_count]
    real_rest = real_kernel[:, skel_count:]
    imag_rest = imag_kernel[:, skel_count:]
    matmul_dims = (((1,), (0,)), ((), ()))
    outer_dims = (((1,), (1,)), ((), ()))

    def product(left_side, right_side):
        return lax.dot_general(
            left_side,
            right_side,
            matmul_dims,
            precision=highest,
            preferred_element_type=jnp.float32,
        )

    def outer_product(left_side, right_side):
        return lax.dot_general(
            left_side, right_side, outer_dims, precision=highest, preferred_element_type=jnp.float32
        )

    real_block = real_rest - (
        product(real_skel, coefficients[0]) - product(imag_skel, coefficients[1])
    )
    imag_block = imag_rest - (
        product(real_skel, coefficients[1]) + product(imag_skel, coefficients[0])
    )
    real_weighted = real_block * pivot_row[0][None, :] - imag_block * pivot_row[1][None, :]
    imag_weighted = real_block * pivot_row[1][None, :] + imag_block * pivot_row[0][None, :]
    real_update = outer_product(real_weighted, real_block) - outer_product(
        imag_weighted, imag_block
    )
    imag_update = outer_product(real_weighted, imag_block) + outer_product(
        imag_weighted, real_block
    )
    return -jnp.stack([real_update, imag_update])


def on_device(
    box_points, proxy_directions, point_order, neighbour_boxes, neighbour_places, pivot_inverse
):
    box_count = box_points.shape[0]
    point_count = box_points.shape[2]
    skel_count = S
    rest_width = pivot_inverse.shape[2]
    col_count = lax.axis_size("col")
    col_index = lax.axis_index("col")
    box_index = lax.axis_index("box")
    box_total = lax.axis_size("box")
    ordered = jnp.take_along_axis(
        box_points, jnp.broadcast_to(point_order[:, None, :], box_points.shape), axis=2
    )
    extended = padded(ordered, (("box", 0),), box_count)
    owner_device = neighbour_boxes // box_count
    device_step = jnp.mod(owner_device - box_index + 1, box_total) - 1
    local_slot = (device_step + 1) * box_count + neighbour_boxes % box_count
    shift_table = decode(neighbour_places)
    proxies = 0.5 + proxy_radius * proxy_directions
    group_size = neighbour_boxes.shape[1] // col_count

    def cross_one(which_box):
        own_points = ordered[which_box]
        slot_rows = lax.dynamic_slice_in_dim(
            local_slot[which_box], col_index * group_size, group_size, 0
        )
        shift_rows = lax.dynamic_slice_in_dim(
            shift_table[which_box], col_index * group_size, group_size, 0
        )
        near_points = extended[slot_rows] + shift_rows[:, :, None]
        near_points = jnp.transpose(near_points, (1, 0, 2)).reshape(3, group_size * point_count)
        targets = jnp.concatenate([proxies, near_points], axis=1)
        real_tile, imag_tile = helmholtz(targets, own_points)
        return cross_products(
            real_tile.astype(jnp.bfloat16), imag_tile.astype(jnp.bfloat16), skel_count
        )

    cross_terms = lax.map(cross_one, jnp.arange(box_count, dtype=jnp.int32))
    gram_total = lax.psum(cross_terms[:, :, :, :skel_count], "col")
    rest_terms = lax.psum_scatter(
        cross_terms[:, :, :, skel_count:], "col", scatter_dimension=3, tiled=True
    )
    factors = jax.vmap(factor)(gram_total)
    interpolation = jax.vmap(apply_inverse)(factors, rest_terms)
    own_start = skel_count + col_index * rest_width
    slot_range = jnp.arange(3 * box_count, dtype=jnp.int32)

    def schur_box(which_box, buffer):
        own_points = ordered[which_box]
        own_columns = jnp.concatenate(
            [
                own_points[:, :skel_count],
                lax.dynamic_slice_in_dim(own_points, own_start, rest_width, 1),
            ],
            axis=1,
        )
        near_points = (
            extended[local_slot[which_box]][:, :, :skel_count] + shift_table[which_box][:, :, None]
        )
        coefficients = interpolation[which_box]
        pivot_row = pivot_inverse[which_box]
        updates = jax.vmap(
            lambda points_one: pair_update(points_one, own_columns, coefficients, pivot_row)
        )(near_points)
        one_hot = (local_slot[which_box][:, None] == slot_range[None, :]).astype(jnp.float32)
        return buffer + jnp.einsum("ks,kcij->scij", one_hot, updates, precision=highest)

    buffer = lax.fori_loop(
        0, box_count, schur_box, jnp.zeros((3 * box_count, 2, skel_count, skel_count), jnp.float32)
    )
    outgoing = jnp.concatenate([buffer[:box_count], buffer[2 * box_count :]], axis=0)
    arrived = padded(outgoing, (("box", 0),), box_count)
    collected = buffer[box_count : 2 * box_count] + arrived[:box_count] + arrived[3 * box_count :]
    skeleton_update = lax.psum_scatter(collected, "col", scatter_dimension=2, tiled=True)
    return (interpolation, skeleton_update)


def solution(mesh):
    placed = (
        P("box", None, None),
        P(None, "col"),
        P("box", None),
        P("box", None),
        P("box", None),
        P("box", None, "col"),
    )
    return jax.shard_map(
        on_device,
        mesh=mesh,
        in_specs=placed,
        out_specs=(P("box", None, None, "col"), P("box", None, "col", None)),
        check_vma=False,
    )
```

profile of v0, /device:TPU:2, one launch (start us, length us, event | category | flops | bytes accessed | tf_op | source)
XLA Modules:
  0.0 602.5 jit_solution(5306556644686090678)
XLA Ops:
  9.4 30.1 %gather_fusion.2 = f32[3072]{0:T(1024)S(1)} fusion(f32[2,3,512]{2,0,1:T(2,128)S(1)} %copy-done, s32[3072]{0:T(1024)S(1)} %reshape.250), kind=kCustom, calls=%fused_computation.2 | custom fusion | bytes 61440 | tf_op jit(solution)/shard_map/jit(take_along_axis)/gather | solution.py:131
  39.5 7.8 %collective-permute-start.1 = (f32[2,3,512]{2,1,0:T(4,128)S(1)}, f32[2,3,512]{2,1,0:T(4,128)S(1)}, u32[]{:S(2)}, u32[]{:S(2)}) collective-permute-start(f32[2,3,512]{2,1,0:T(4,128)S(1)} %fusion.118), channel_id=1, source_target_pairs={{4,0},{8,4},{12,8},{16,12},{20,16},{24,20},{28,24},{32,28},{36,32}... | collective-permute-start | bytes 36872 | tf_op jit(solution)/shard_map/ppermute | solution.py:27
  48.8 5.0 collective-permute-done
  53.8 58.9 %while.31 = (s32[]{:T(128)}, f32[2,2,256,512]{3,2,1,0:T(8,128)S(1)}, s32[2]{0:T(128)S(1)}, s32[2,8]{1,0:T(2,128)S(1)}, s32[]{:T(128)}, /*index=5*/f32[6,3,512]{2...) while((s32[]{:T(128)}, ...), condition=%wide.region_1.2_spmd, body=%wide.region_0.0_spmd.sunk | while | flops 1378492160 | bytes 13771115 | solution.py:158
  57.2 11.7 %fusion.183 = bf16[1280,512]{1,0:T(8,128)(2,1)S(1)} fusion(f32[512]{0:T(512)S(1)} %bitcast.240, f32[1280]{0:T(1024)S(1)} %get-tuple-element.827, f32[512]{0:T(512)S(1)} %bitcast.238, f32[1280]{0:T(1024)S(1)} %get-tuple-element.829, f32[512]{0:T(512)S(1)} %bitcast.236, f32[1280]{0:T(1024)S(1)} %get-tuple-element.831), kind=kLoop, calls=%fused_computation.40.clone.1 | loop fusion | flops 10485760 | bytes 1332224 | tf_op jit(solution)/shard_map/while/body/eval_jaxpr/neg | solution.py:51
  68.9 12.6 %multiply_convert_fusion.3 = (bf16[1280,512]{1,0:T(8,128)(2,1)S(1)}, bf16[1280,512]{1,0:T(8,128)(2,1)S(1)}) fusion(f32[512]{0:T(512)S(1)} %bitcast.241, f32[1280]{0:T(1024)S(1)} %get-tuple-element.827, f32[512]{0:T(512)S(1)} %bitcast.239, f32[1280]{0:T(1024)S(1)} %get-tuple-element.829, f32[512]{0:T(512)S(1)} %bitcast.237, ...), kind=kLoop, calls=%fused_computation.15.clone.2 | loop fusion | flops 9830400 | bytes 2642944 | tf_op jit(solution)/shard_map/while/body/eval_jaxpr/convert_element_type | solution.py:155
  86.6 11.7 %fusion.183 = bf16[1280,512]{1,0:T(8,128)(2,1)S(1)} fusion(f32[512]{0:T(512)S(1)} %bitcast.240, f32[1280]{0:T(1024)S(1)} %get-tuple-element.827, f32[512]{0:T(512)S(1)} %bitcast.238, f32[1280]{0:T(1024)S(1)} %get-tuple-element.829, f32[512]{0:T(512)S(1)} %bitcast.236, f32[1280]{0:T(1024)S(1)} %get-tuple-element.831), kind=kLoop, calls=%fused_computation.40.clone.1 | loop fusion | flops 10485760 | bytes 1332224 | tf_op jit(solution)/shard_map/while/body/eval_jaxpr/neg | solution.py:51
  98.3 12.6 %multiply_convert_fusion.3 = (bf16[1280,512]{1,0:T(8,128)(2,1)S(1)}, bf16[1280,512]{1,0:T(8,128)(2,1)S(1)}) fusion(f32[512]{0:T(512)S(1)} %bitcast.241, f32[1280]{0:T(1024)S(1)} %get-tuple-element.827, f32[512]{0:T(512)S(1)} %bitcast.239, f32[1280]{0:T(1024)S(1)} %get-tuple-element.829, f32[512]{0:T(512)S(1)} %bitcast.237, ...), kind=kLoop, calls=%fused_computation.15.clone.2 | loop fusion | flops 9830400 | bytes 2642944 | tf_op jit(solution)/shard_map/while/body/eval_jaxpr/convert_element_type | solution.py:155
  112.7 1.9 copy.171
  114.6 2.4 copy.180
  117.0 2.5 slice.434
  122.4 56.0 %all-reduce.5.cloned.1.call-done = (f32[2,2,256,256]{2,3,0,1:T(8,128)}, f32[2,2,256,256]{2,1,0,3:T(2,128)}) async-done(((f32[2,2,256,256]{2,3,0,1:T(8,128)}, f32[2,2,256,256]{2,1,0,3:T(2,128)}), (f32[2,2,256,256]{2,3,0,1:T(8,128)}, f32[2,2,256,256]{2,1,0,3:T(2,128)})) %all-reduce.5.cloned.1.call-update) | async-done | bytes 2097168 | tf_op jit(solution)/shard_map/psum | solution.py:159
  178.4 1.9 slice_bitcast_fusion.2
  185.1 2.1 copy.172
  187.2 2.1 fusion.72
  190.6 23.5 %custom-call.36 = f32[2,128,128]{2,1,0:T(8,128)S(1)} custom-call(f32[2,128,128]{2,1,0:T(8,128)S(1)} %cholesky.274), custom_call_target="Cholesky" | custom-call | tf_op jit(solution)/shard_map/vmap(jit(cholesky))/cholesky | solution.py:67
  214.1 19.7 %custom-call.37 = f32[2,1,128,128]{2,3,1,0:T(8,128)S(1)} custom-call(f32[2,1,128,128]{3,2,1,0:T(8,128)S(1)} %select_bitcast_fusion.2), custom_call_target="InvertDiagBlocksLowerTriangular" | custom-call | tf_op jit(solution)/shard_map/vmap(jit(cholesky))/cholesky | solution.py:67
  234.0 1.5 constant_dynamic-update-slice_fusion.3
  235.6 1.5 convolution_subtract_fusion
  237.1 23.5 %custom-call.38 = f32[2,128,128]{2,1,0:T(8,128)S(1)} custom-call(f32[2,128,128]{2,1,0:T(8,128)S(1)} %cholesky.278), custom_call_target="Cholesky" | custom-call | tf_op jit(solution)/shard_map/vmap(jit(cholesky))/cholesky | solution.py:67
  260.6 20.1 %custom-call.39 = f32[2,1,128,128]{2,3,1,0:T(8,128)S(1)} custom-call(f32[2,1,128,128]{3,2,1,0:T(8,128)S(1)} %get-tuple-element.671), custom_call_target="InvertDiagBlocksLowerTriangular" | custom-call | tf_op jit(solution)/shard_map/vmap(jit(cholesky))/cholesky | solution.py:67
  281.0 1.6 convolution_subtract_fusion.1
  282.6 23.5 %custom-call.40 = f32[2,128,128]{2,1,0:T(8,128)S(1)} custom-call(f32[2,128,128]{2,1,0:T(8,128)S(1)} %cholesky.283), custom_call_target="Cholesky" | custom-call | tf_op jit(solution)/shard_map/vmap(jit(cholesky))/cholesky | solution.py:67
  306.1 19.7 %custom-call.41 = f32[2,1,128,128]{2,3,1,0:T(8,128)S(1)} custom-call(f32[2,1,128,128]{3,2,1,0:T(8,128)S(1)} %get-tuple-element.669), custom_call_target="InvertDiagBlocksLowerTriangular" | custom-call | tf_op jit(solution)/shard_map/vmap(jit(cholesky))/cholesky | solution.py:67
  326.1 1.5 convolution_subtract_fusion.2
  327.6 23.7 %custom-call.42 = f32[2,128,128]{2,1,0:T(8,128)S(1)} custom-call(f32[2,128,128]{2,1,0:T(8,128)S(1)} %convolution_subtract_fusion.2), custom_call_target="Cholesky" | custom-call | tf_op jit(solution)/shard_map/vmap(jit(cholesky))/cholesky | solution.py:67
  351.7 1.7 select_select_fusion
  353.4 14.5 %while.32 = (s32[]{:T(128)}, f32[2,512,512]{2,1,0:T(8,128)}, s32[4,2]{0,1:T(2,128)S(1)}, f32[4,2,128,128]{3,2,0,1:T(8,128)}, s32[]{:T(128)}) while((s32[]{:T(128)}, f32[2,512,512]{2,1,0:T(8,128)}, s32[4,2]{0,1:T(2,128)S(1)}, f32[4,2,128,128]{3,2,0,1:T(8,128)}, s32[]{:T(128)}) %tuple.147), condition=%wide.while_cond, body=%wide.while_body.sunk | while | flops 2 | bytes 263277 | solution.py:73
  354.0 3.0 bitcast_dynamic-update-slice_fusion.2
  357.7 3.0 bitcast_dynamic-update-slice_fusion.2
  361.3 3.0 bitcast_dynamic-update-slice_fusion.2
  364.9 2.9 bitcast_dynamic-update-slice_fusion.2
  367.9 79.4 %custom-call.43 = f32[2,4,128,128]{2,3,1,0:T(8,128)S(1)} custom-call(f32[2,4,128,128]{3,2,1,0:T(8,128)} %bitcast.242), custom_call_target="InvertDiagBlocksLowerTriangular" | custom-call | tf_op jit(solution)/shard_map/vmap()/triangular_solve | solution.py:73
  450.8 1.6 convolution_subtract_fusion.8
  456.2 1.4 convolution_subtract_fusion.7
  458.0 89.5 %while.33 = (s32[]{:T(128)}, f32[6,2,256,256]{3,0,2,1:T(8,128)}, s32[2,8]{1,0:T(2,128)S(1)}, f32[6,3,512]{2,1,0:T(4,128)S(1)}, f32[2,8,3]{1,0,2:T(2,128)S(1)}, /...) while((s32[]{:T(128)}, f32[6,2,256,256]{3,0,2,1:T(8,128)}, ...), condition=%wide.region_14.15_spmd.clone, body=%wide.region_13.14_spmd.clone.sunk | while | flops 3312066560 | bytes 79216528 | solution.py:188
  478.7 10.8 %cosine_multiply_fusion.2 = (f32[8,256,320]{1,2,0:T(8,128)S(1)}, f32[8,256,320]{1,2,0:T(8,128)S(1)}) fusion(f32[320]{0:T(512)S(1)} %get-tuple-element.849, f32[8,256]{1,0:T(8,128)S(1)} %get-tuple-element.852, f32[320]{0:T(512)S(1)} %get-tuple-element.853, f32[8,256]{1,0:T(8,128)S(1)} %get-tuple-element.854, f32[320]{0:T(512)S(1)} %get-tuple-element.855, ...), kind=kLoop, calls=%fused_computation.47.clone.1 | loop fusion | flops 8519680 | bytes 5271296 | tf_op jit(solution)/shard_map/while/body/eval_jaxpr/vmap()/mul | solution.py:39
  489.5 1.5 fusion.202
  491.0 1.5 fusion.203
  492.5 1.5 fusion.200
  494.0 1.5 fusion.201
  495.5 1.9 fusion.205
  497.4 2.0 subtract_bitcast_fusion.2
  499.4 1.9 fusion.204
  501.4 2.0 add_bitcast_fusion.3
  503.8 1.8 copy-done.2
  505.6 5.0 select_add_fusion.2
  510.6 1.9 copy-done.3
  513.5 10.8 %cosine_multiply_fusion.2 = (f32[8,256,320]{1,2,0:T(8,128)S(1)}, f32[8,256,320]{1,2,0:T(8,128)S(1)}) fusion(f32[320]{0:T(512)S(1)} %get-tuple-element.849, f32[8,256]{1,0:T(8,128)S(1)} %get-tuple-element.852, f32[320]{0:T(512)S(1)} %get-tuple-element.853, f32[8,256]{1,0:T(8,128)S(1)} %get-tuple-element.854, f32[320]{0:T(512)S(1)} %get-tuple-element.855, ...), kind=kLoop, calls=%fused_computation.47.clone.1 | loop fusion | flops 8519680 | bytes 5271296 | tf_op jit(solution)/shard_map/while/body/eval_jaxpr/vmap()/mul | solution.py:39
  524.3 1.5 fusion.202
  525.8 1.5 fusion.203
  527.3 1.5 fusion.200
  528.8 1.5 fusion.201
  530.3 1.9 fusion.205
  532.2 2.0 subtract_bitcast_fusion.2
  534.3 1.9 fusion.204
  536.2 2.0 add_bitcast_fusion.3
  538.6 1.8 copy-done.2
  540.4 5.0 select_add_fusion.2
  545.5 1.9 copy-done.3
  547.6 3.3 copy.192
  551.2 5.0 collective-permute-start.3
  556.3 12.5 %collective-permute-done.2 = f32[2,2,256,256]{3,2,1,0:T(8,128)S(1)} collective-permute-done((f32[2,2,256,256]{3,2,1,0:T(8,128)S(1)}, f32[2,2,256,256]{3,2,1,0:T(8,128)S(1)}, u32[]{:S(2)}, u32[]{:S(2)}) %collective-permute-start.2) | collective-permute-done | bytes 1048608 | tf_op jit(solution)/shard_map/ppermute | solution.py:24
  570.0 25.3 %reduce-scatter.2.cloned.1.call-done = f32[2,2,64,256]{3,2,1,0:T(8,128)} async-done(((f32[2,2,256,256]{3,2,1,0:T(8,128)}), f32[2,2,64,256]{3,2,1,0:T(8,128)}) %reduce-scatter.2.cloned.1.call-update) | async-done | bytes 262160 | tf_op jit(solution)/shard_map/reduce_scatter | solution.py:194
  (171 shorter events, 33.8 us)
Async XLA Ops:
  7.2 2.2 copy-start
  7.2 171.2 %all-reduce.5.cloned.1.call-start = ((), (), s32[]{:S(2)}) async-start(), calls=%async_computation.2 | async-start | bytes 4194304 | tf_op jit(solution)/shard_map/psum | solution.py:159
  9.3 30.1 %copy-start.12 = (s32[2,512]{1,0:T(2,128)S(1)}, s32[2,512]{1,0:T(2,128)}, u32[]{:S(2)}) copy-start(s32[2,512]{1,0:T(2,128)} %param.12) | copy-start | bytes 12292
  9.4 38.0 %copy-start.16 = (s32[2,8]{1,0:T(2,128)S(1)}, s32[2,8]{1,0:T(2,128)}, u32[]{:S(2)}) copy-start(s32[2,8]{1,0:T(2,128)} %param.14) | copy-start | bytes 196
  9.4 38.0 %copy-start.14 = (f32[3,256]{1,0:T(4,128)S(1)}, f32[3,256]{1,0:T(4,128)}, u32[]{:S(2)}) copy-start(f32[3,256]{1,0:T(4,128)} %param.11) | copy-start | bytes 9220
  9.4 38.0 %copy-start.15 = (s32[2,8]{1,0:T(2,128)S(1)}, s32[2,8]{1,0:T(2,128)}, u32[]{:S(2)}) copy-start(s32[2,8]{1,0:T(2,128)} %param.13) | copy-start | bytes 196
  39.5 9.3 %collective-permute-start.1 = (f32[2,3,512]{2,1,0:T(4,128)S(1)}, f32[2,3,512]{2,1,0:T(4,128)S(1)}, u32[]{:S(2)}, u32[]{:S(2)}) collective-permute-start(f32[2,3,512]{2,1,0:T(4,128)S(1)} %fusion.118), channel_id=1, source_target_pairs={{4,0},{8,4},{12,8},{16,12},{20,16},{24,20},{28,24},{32,28},{36,32}... | collective-permute-start | bytes 36872 | tf_op jit(solution)/shard_map/ppermute | solution.py:27
  47.3 6.5 %collective-permute-start = (f32[2,3,512]{2,1,0:T(4,128)S(1)}, f32[2,3,512]{2,1,0:T(4,128)S(1)}, u32[]{:S(2)}, u32[]{:S(2)}) collective-permute-start(f32[2,3,512]{2,1,0:T(4,128)S(1)} %fusion.118), channel_id=1, source_target_pairs={{0,4},{4,8},{8,12},{12,16},{16,20},{20,24},{24,28},{28,32},{32,36}... | collective-permute-start | bytes 36872 | tf_op jit(solution)/shard_map/ppermute | solution.py:24
  117.0 2.5 copy-start.6
  119.5 1.5 copy-start.17
  120.9 474.4 %reduce-scatter.2.cloned.1.call-start = ((), (), s32[]{:S(2)}) async-start(), calls=%async_computation.1 | async-start | bytes 1310720 | tf_op jit(solution)/shard_map/reduce_scatter | solution.py:194
  178.4 5.2 copy-start.7
  189.3 1.3 copy-start.5
  351.6 95.7 %copy-start.9 = (f32[2,128,64]{1,0,2:T(2,128)S(1)}, f32[2,128,64]{1,0,2:T(2,128)}, u32[]{:S(2)}) copy-start(f32[2,128,64]{1,0,2:T(2,128)} %get-tuple-element.667) | copy-start | bytes 196612
  351.6 95.9 %copy-start.8 = (f32[2,128,64]{1,0,2:T(2,128)S(1)}, f32[2,128,64]{1,0,2:T(2,128)}, u32[]{:S(2)}) copy-start(f32[2,128,64]{1,0,2:T(2,128)} %get-tuple-element.666) | copy-start | bytes 196612
  353.4 95.8 %copy-start.11 = (f32[2,128,64]{1,0,2:T(2,128)S(1)}, f32[2,128,64]{1,0,2:T(2,128)}, u32[]{:S(2)}) copy-start(f32[2,128,64]{1,0,2:T(2,128)} %get-tuple-element.665) | copy-start | bytes 196612
  353.4 97.4 %copy-start.10 = (f32[2,128,64]{1,0,2:T(2,128)S(1)}, f32[2,128,64]{1,0,2:T(2,128)}, u32[]{:S(2)}) copy-start(f32[2,128,64]{1,0,2:T(2,128)} %get-tuple-element.664) | copy-start | bytes 196612
  452.4 5.6 copy-start.13
  503.4 2.2 copy-start.2
  510.6 1.9 copy-start.3
  538.2 2.2 copy-start.2
  545.5 1.9 copy-start.3
  547.6 3.3 copy-start.4
  551.1 17.6 %collective-permute-start.2 = (f32[2,2,256,256]{3,2,1,0:T(8,128)S(1)}, f32[2,2,256,256]{3,2,1,0:T(8,128)S(1)}, u32[]{:S(2)}, u32[]{:S(2)}) collective-permute-start(f32[2,2,256,256]{3,2,1,0:T(8,128)S(1)} %get-tuple-element.660), channel_id=1, source_target_pairs={{0,4},{4,8},{8,12},{12,16},{16,20},{20,24},{24,28},{28,32},{32,36}... | collective-permute-start | bytes 3145736 | tf_op jit(solution)/shard_map/ppermute | solution.py:24
  551.2 44.0 %copy-start.1 = (f32[2,3,512]{2,0,1:T(2,128)S(1)}, f32[2,3,512]{2,0,1:T(2,128)}, u32[]{:S(2)}) copy-start(f32[2,3,512]{2,0,1:T(2,128)} %param.10) | copy-start | bytes 36868
  551.2 17.5 %collective-permute-start.3 = (f32[2,2,256,256]{3,2,1,0:T(8,128)S(1)}, f32[2,2,256,256]{3,2,1,0:T(8,128)S(1)}, u32[]{:S(2)}, u32[]{:S(2)}) collective-permute-start(f32[2,2,256,256]{3,2,1,0:T(8,128)S(1)} %get-tuple-element.661), channel_id=1, source_target_pairs={{4,0},{8,4},{12,8},{16,12},{20,16},{24,20},{28,24},{32,28},{36,32}... | collective-permute-start | bytes 3145736 | tf_op jit(solution)/shard_map/ppermute | solution.py:27
Sparse Core Ops, SparseCore 0:
  121.0 57.3 all-reduce.4
  570.1 25.1 reduce-scatter.1
where the time goes:
time: 612 us; the launch traced here: 602 us
  other arithmetic  315 us (51%)
  waiting for transfers between devices  100 us (16%)
  local copies, waits for them, and re-layouts  76.2 us (12%)
  matrix products  58.5 us (10%)
  loops' own time  24.1 us (4%)
  between operations  15.7 us (3%)
  starting transfers between devices  13 us (2%)
    another operation x16, other arithmetic, factor(): jnp.linalg.cholesky(jnp.concatenate([upper_half, lower_half], axis=0))  154 us
    another operation x5, other arithmetic, apply_inverse(): lax.linalg.triangular_solve(cholesky_factor, forward, left_side=True, low...  81.2 us
    psum x1, waiting for transfers between devices, on_device(): gram_total = lax.psum(cross_terms[:, :, :, :skel_count], 'col')  56 us
    gather x3, local copies, waits for them, and re-layouts, on_device(): jnp.take_along_axis(box_points, jnp.broadcast_to(point_order[:, None, :],...  30.1 us
    reduce_scatter x1, waiting for transfers between devices, on_device(): lax.psum_scatter(collected, 'col', scatter_dimension=2, tiled=True)  25.3 us
    convert_element_type x2, other arithmetic, cross_one(): real_tile.astype(jnp.bfloat16)  25.2 us
    neg x2, other arithmetic, cross_products(): flipped = jnp.concatenate([imag_tile, -real_tile], axis=0)  23.3 us
    mul x2, other arithmetic, helmholtz(): amplitude * jnp.cos(wavenumber * radius)  21.5 us
  transfers between devices with their start and end apart: 6, of which 5 were waited for; matrix products, arithmetic and copies ran while one was open for 0% of the time, Pallas kernels for 0%

commit v1 on v0

v1 whole, which is shorter than its diff:
```python
import math

import jax
import jax.numpy as jnp
import numpy as np
from jax import lax
from jax.experimental import pallas as pl
from jax.experimental.pallas import tpu as pltpu
from jax.sharding import PartitionSpec as P

S = 256
H = 64
NBR = 8
NBOX = 2
f32 = jnp.float32
bf16 = jnp.bfloat16
softening = 0.05
ridge_share = 0.05


def chebyshev_fit(function, count):
    nodes = 0.125 + 0.125 * np.cos(np.pi * (np.arange(256) + 0.5) / 256)
    fit = np.polynomial.chebyshev.Chebyshev.fit(nodes, function(np.sqrt(nodes)), count - 1, domain=[0, 0.25])
    return [float(c) for c in fit.convert(kind=np.polynomial.Polynomial).coef]


SIN_COEF = chebyshev_fit(lambda g: np.sin(np.pi * g) / (g * math.sqrt(math.pi)), 5)
COS_COEF = chebyshev_fit(lambda g: np.cos(np.pi * g) / math.sqrt(math.pi), 5)


def horner(z, coef):
    out = coef[-1]
    for c in coef[-2::-1]:
        out = out * z + c
    return out


def split2(x):
    high = x.astype(bf16)
    return high, (x - high.astype(f32)).astype(bf16)


def split3(x):
    high = x.astype(bf16).astype(f32)
    rest = x - high
    middle = rest.astype(bf16).astype(f32)
    return high, middle, (rest - middle).astype(bf16).astype(f32)


def dot(a, b, rhs_transposed=False, precision=None):
    dims = (((1,), (1 if rhs_transposed else 0,)), ((), ()))
    return lax.dot_general(a, b, dims, precision=precision, preferred_element_type=f32)


def turned(x):
    swapped = pltpu.roll(x, x.shape[1] // 2, 1)
    lane = lax.broadcasted_iota(jnp.int32, x.shape, 1)
    return jnp.where(lane < x.shape[1] // 2, -swapped, swapped)


def expand(x):
    return jnp.concatenate([x, turned(x)], axis=0)


def evaluate(v):
    inv = lax.rsqrt(v)
    turns = v * inv
    g = turns - jnp.round(turns)
    z = g * g
    s = g * horner(z, SIN_COEF)
    c = horner(z, COS_COEF)
    return inv * (1.0 / (2.0 * math.pi) - s * s), inv * (s * c)


def invert(w):
    row_id = lax.broadcasted_iota(jnp.int32, w.shape, 0)
    lane_id = lax.broadcasted_iota(jnp.int32, w.shape, 1)
    line_id = lax.broadcasted_iota(jnp.int32, (1, 2 * H), 1)
    col_id = lax.broadcasted_iota(jnp.int32, (H, 1), 0)
    for k in range(H):
        col_re = w[:, k : k + 1]
        col_im = w[:, H + k : H + k + 1]
        pivot = 1.0 / col_re[k : k + 1]
        row = w[k : k + 1] * pivot
        row = jnp.where(line_id == k, pivot, jnp.where(line_id == H + k, 0.0, row))
        row_turned = turned(row)
        kept = jnp.where((row_id == k) | (lane_id == k) | (lane_id == H + k), 0.0, w)
        col_re = jnp.where(col_id == k, -1.0, col_re)
        col_im = jnp.where(col_id == k, 0.0, col_im)
        w = kept - col_re * row - col_im * row_turned
    return w


def kernel(
    boxes_ref, places_ref, own_ref, before_ref, after_ref, shared_ref,
    interp_ref, update_ref,
    point_ref, source_ref, target_ref, rhs_ref, rest_ref, low_ref, rest_low_ref, z_ref, q_ref,
):
    me = lax.axis_index("box")
    col = lax.axis_index("col")
    total = lax.axis_size("box")
    highest = lax.Precision.HIGHEST

    row8 = lax.broadcasted_iota(jnp.int32, (8, 512), 0)
    for slot in range(6):
        ref = (before_ref, own_ref, after_ref)[slot // 2]
        data = ref[slot % 2]
        order = data[3:4]
        pick = (lax.broadcasted_iota(jnp.int32, (512, 512), 0).astype(f32) == order).astype(bf16)
        parts = split3(2.0 * data - 1.0)
        got = dot(jnp.concatenate(parts + (jnp.zeros_like(data),), axis=0).astype(bf16), pick)
        points = jnp.where(row8[:4] < 3, (got[0:4] + got[4:8]) + got[8:12], 0.0)
        point_ref[slot, 0:4] = points
        point_ref[slot, 4:8] = jnp.zeros_like(points)

    def features(points, is_source):
        width = points.shape[1]
        rows = row8[:, :width]
        square = jnp.sum(points * points, axis=0, keepdims=True)
        if is_source:
            square = square + 4.0 * softening * softening
            scaled = points
        else:
            scaled = -2.0 * points
        high, middle, low = split3(scaled)
        groups = (high, high, middle, high, low, middle) if is_source else (high, middle, high, low, high, middle)
        own_row, other_row = (4, 3) if is_source else (3, 4)
        out = []
        for i, group in enumerate(groups):
            if i < 3:
                part = split3(square)[i]
                group = jnp.where(rows == own_row, part, jnp.where(rows == other_row, 1.0, group))
            out.append(group)
        return jnp.concatenate(out, axis=0)

    for b in range(NBOX):
        source_ref[b] = features(point_ref[2 + b], True).T.astype(bf16)

    slots = []
    back = lax.rem(S - H * col, S)
    for p in range(NBOX * NBR):
        b, k = p // NBR, p % NBR
        box = boxes_ref[b, k]
        code = places_ref[b, k]
        code = code + (code >= 13).astype(jnp.int32)
        step = lax.rem((box >> 1) - me + 1 + total, total)
        slot = step * 2 + (box & 1)
        slots.append(slot)
        dx = (2 * (code // 9) - 2).astype(f32)
        dy = (2 * (code // 3 % 3) - 2).astype(f32)
        dz = (2 * (code % 3) - 2).astype(f32)
        move = jnp.where(row8 == 0, dx, jnp.where(row8 == 1, dy, jnp.where(row8 == 2, dz, 0.0)))
        got = features(point_ref[slot] + move, False)
        target_ref[p] = pltpu.roll(got[:, :S], back, 1).astype(bf16)
        target_ref[16 + p] = got[:, S:].astype(bf16)
    for d in range(4):
        data = shared_ref[d]
        points = jnp.concatenate([jnp.where(row8[:4, :S] < 3, 3.0 * data, 0.0), jnp.zeros_like(data)], axis=0)
        target_ref[32 + d] = features(points, False).astype(bf16)

    flat = jnp.concatenate([shared_ref[d, 3:4] for d in range(4)] + [jnp.zeros((4, S), f32)], axis=0).T
    for b in range(NBOX):
        for part in range(2):
            for d in range(4):
                first = (2 * b + part) * H
                q_ref[b, part, d * H : (d + 1) * H] = jnp.broadcast_to(flat[first : first + H, d : d + 1], (H, 128))

    def tile(b, chunk, keep, place):
        features_t = target_ref[chunk]
        for g in range(8):
            re, im = evaluate(dot(source_ref[b, g * H : (g + 1) * H], features_t))
            re_high, im_high = re.astype(bf16), im.astype(bf16)
            if g < 4:
                top = slice(2 * H * g, 2 * H * g + H)
                bottom = slice(2 * H * g + H, 2 * H * (g + 1))
                rhs_ref[place, top, :S] = re_high
                rhs_ref[place, top, S:] = im_high
                rhs_ref[place, bottom, :S] = -im_high
                rhs_ref[place, bottom, S:] = re_high
            else:
                span = slice(H * (g - 4), H * (g - 3))
                rest_ref[place, span, :S] = re_high
                rest_ref[place, span, S:] = im_high
            if keep:
                re_low = (re - re_high.astype(f32)).astype(bf16)
                im_low = (im - im_high.astype(f32)).astype(bf16)
                if g < 4:
                    low_ref[place, top, :S] = re_low
                    low_ref[place, top, S:] = im_low
                    low_ref[place, bottom, :S] = -im_low
                    low_ref[place, bottom, S:] = re_low
                else:
                    rest_low_ref[place, span, :S] = re_low
                    rest_low_ref[place, span, S:] = im_low
        left = jnp.concatenate(
            [rhs_ref[place, 2 * H * g : 2 * H * g + H] for g in range(4)] + [rest_ref[place]], axis=0
        )
        got = dot(left, rhs_ref[place], rhs_transposed=True)
        for c in range(4):
            z_ref[b, c] += got[:, 2 * H * c : 2 * H * (c + 1)]

    z_ref[...] = jnp.zeros_like(z_ref)
    for b in range(NBOX):

        @pl.loop(0, NBR)
        def _(k):
            tile(b, b * NBR + k, True, b * NBR + k)

        @pl.loop(0, NBR + 4)
        def _(k):
            tile(b, jnp.where(k < NBR, 16 + b * NBR + k, 24 + k), False, 16)

    for b in range(NBOX):
        row_id = lax.broadcasted_iota(jnp.int32, (H, 2 * H), 0)
        lane_id = lax.broadcasted_iota(jnp.int32, (H, 2 * H), 1)
        on_diagonal = row_id == lane_id
        trace = jnp.zeros((1, 1), f32)
        for c in range(4):
            block = jnp.where(on_diagonal, z_ref[b, c, c * H : (c + 1) * H], 0.0)
            trace = trace + jnp.sum(jnp.sum(block, axis=0, keepdims=True), axis=1, keepdims=True)
        ridge = jnp.where(on_diagonal, ridge_share * trace / S, 0.0)
        for c in range(4):
            z_ref[b, c, c * H : (c + 1) * H] += ridge

    @pl.loop(0, 4)
    def _(kb):
        rows = pl.ds(pl.multiple_of(kb * H, H), H)
        inverses = [invert(z_ref[b, kb, rows]) for b in range(NBOX)]
        for b in range(NBOX):
            block = dot(z_ref[b, kb], expand(inverses[b]), precision=highest)
            z_ref[b, kb] = block
            for t in range(1, 4):
                c = lax.rem(kb + t, 4)
                z_ref[b, c] -= dot(block, expand(z_ref[b, c, rows]), precision=highest)

    mine = pl.ds(pl.multiple_of(col * H, H), H)
    for b in range(NBOX):
        for c in range(4):
            across = z_ref[b, c, pl.ds(pl.multiple_of(S + col * H, H), H)].T
            interp_ref[b, 0, c * H : (c + 1) * H] = across[:H]
            interp_ref[b, 1, c * H : (c + 1) * H] = across[H:]

    update_ref[...] = jnp.zeros_like(update_ref)
    for b in range(NBOX):
        x = jnp.concatenate([z_ref[b, c, S:] for c in range(4)], axis=1)
        x_high, x_low = split2(x)
        x_both = jnp.concatenate([x_high, x_low], axis=0)
        for k in range(NBR):
            p = b * NBR + k
            both = dot(x_both, rhs_ref[p])
            block = (rest_ref[p].astype(f32) + rest_low_ref[p].astype(f32)) - (
                (both[:S] + both[S:]) + dot(x_high, low_ref[p])
            )
            first = jnp.concatenate([block[:, :H], block[:, S : S + H]], axis=1)
            weighted = (q_ref[b, 0] * first + q_ref[b, 1] * turned(first)).T
            left = jnp.concatenate([weighted, jnp.concatenate([-weighted[H:], weighted[:H]], axis=0)], axis=1)
            left_high, left_low = split2(left)
            right = jnp.concatenate([block[:, :S], block[:, S:]], axis=0)
            right_high, right_low = split2(right)
            got = dot(jnp.concatenate([left_high, left_low], axis=0), right_high)
            update_ref[slots[p]] -= (got[: 2 * H] + got[2 * H :]) + dot(left_high, right_low)
    for slot in range(6):
        update_ref[slot] = pltpu.roll(update_ref[slot], H * col, 1)


def on_device(
    box_points, proxy_directions, point_order, neighbour_boxes, neighbour_places, pivot_inverse
):
    count = lax.axis_size("box")
    forward = [(i, (i + 1) % count) for i in range(count)]
    backward = [((i + 1) % count, i) for i in range(count)]
    own = jnp.concatenate([box_points, point_order.astype(f32)[:, None, :]], axis=1)
    before = lax.ppermute(own, "box", forward)
    after = lax.ppermute(own, "box", backward)
    shared = lax.all_gather(
        jnp.concatenate([proxy_directions, pivot_inverse.reshape(1, S)], axis=0), "col"
    )
    smem = pl.BlockSpec(memory_space=pltpu.SMEM)
    vmem = pl.BlockSpec(memory_space=pltpu.VMEM)
    interpolation, update = pl.pallas_call(
        kernel,
        out_shape=(
            jax.ShapeDtypeStruct((NBOX, 2, S, H), f32),
            jax.ShapeDtypeStruct((6, 2 * H, S), f32),
        ),
        in_specs=[smem, smem, vmem, vmem, vmem, vmem],
        out_specs=(vmem, vmem),
        scratch_shapes=[
            pltpu.VMEM((6, 8, 512), f32),
            pltpu.VMEM((NBOX, 512, 48), bf16),
            pltpu.VMEM((36, 48, S), bf16),
            pltpu.VMEM((17, 512, 512), bf16),
            pltpu.VMEM((17, S, 512), bf16),
            pltpu.VMEM((16, 512, 512), bf16),
            pltpu.VMEM((16, S, 512), bf16),
            pltpu.VMEM((NBOX, 4, 512, 2 * H), f32),
            pltpu.VMEM((NBOX, 2, S, 128), f32),
        ],
        compiler_params=pltpu.CompilerParams(vmem_limit_bytes=60 * 1024 * 1024),
        name="skeletonize",
    )(neighbour_boxes, neighbour_places, own, before, after, shared)
    update = update.reshape(6, 2, H, S)
    from_before = lax.ppermute(update[4:6], "box", forward)
    from_after = lax.ppermute(update[0:2], "box", backward)
    return (interpolation, update[2:4] + from_before + from_after)


def solution(mesh):
    placed = (
        P("box", None, None),
        P(None, "col"),
        P("box", None),
        P("box", None),
        P("box", None),
        P("box", None, "col"),
    )
    return jax.shard_map(
        on_device,
        mesh=mesh,
        in_specs=placed,
        out_specs=(P("box", None, None, "col"), P("box", None, "col", None)),
        check_vma=False,
    )
```

time: 612 us -> 162 us (0.26); the launches traced: 602 us -> 161 us
  other arithmetic: 315 us -> 1.47 us
  Pallas kernels: 0 us -> 125 us
  waiting for transfers between devices: 100 us -> 8.23 us
  local copies, waits for them, and re-layouts: 76.2 us -> 3.41 us
  matrix products: 58.5 us -> 0 us
  loops' own time: 24.1 us -> 0 us
  between operations: 15.7 us -> 0.73 us
  blocking collectives: 0 us -> 12.5 us
    another operation x22 -> x0, other arithmetic: 235 us -> none  [the longest x16 154 us: factor(): jnp.linalg.cholesky(jnp.concatenate([upper_half, lower_half], axis=0))]
    pallas_call x0 -> x1, Pallas kernels: none -> 125 us  [on_device(): pl.pallas_call(kernel, out_shape=(jax.ShapeDtypeStruct((NBOX, 2, S, H), f...]
    psum x1 -> x0, waiting for transfers between devices: 56 us -> none  [on_device(): gram_total = lax.psum(cross_terms[:, :, :, :skel_count], 'col')]
    dot_general x22 -> x0, matrix products: 41.2 us -> none  [the longest x8 15.8 us: outer_product(): lax.dot_general(left_side, right_side, outer_dims, precision=highest, pre...]
    gather x7 -> x0, local copies, waits for them, and re-layouts: 32.4 us -> none  [the longest x3 30.1 us: on_device(): jnp.take_along_axis(box_points, jnp.broadcast_to(point_order[:, None, :],...]
    reduce_scatter x1 -> x0, waiting for transfers between devices: 25.3 us -> none  [on_device(): lax.psum_scatter(collected, 'col', scatter_dimension=2, tiled=True)]
    convert_element_type x4 -> x1, other arithmetic: 25.2 us -> 0.7 us  [on_device(): point_order.astype(f32)[:, None, :]]
    another operation x3 -> x0, loops' own time: 24.1 us -> none  [the longest x1 20.1 us: on_device(): lax.fori_loop(0, box_count, schur_box, jnp.zeros((3 * box_count, 2, skel_...]
  transfers between devices with their start and end apart: 6 -> 4, of which waited for: 5 -> 2; matrix products, arithmetic and copies ran while one was open for 0% -> 1% of each run, Pallas kernels for 0% -> 0%
where the time goes in v1:
time: 162 us; the launch traced here: 161 us
  Pallas kernels  125 us (77%)
  blocking collectives  12.5 us (8%)
  starting transfers between devices  10.2 us (6%)
  waiting for transfers between devices  8.23 us (5%)
  local copies, waits for them, and re-layouts  3.41 us (2%)
    pallas_call x1, Pallas kernels, on_device(): pl.pallas_call(kernel, out_shape=(jax.ShapeDtypeStruct((NBOX, 2, S, H), f...  125 us
    all_gather x1, blocking collectives, on_device(): lax.all_gather(jnp.concatenate([proxy_directions, pivot_inverse.reshape(1...  12.5 us
    ppermute x1, starting transfers between devices, on_device(): after = lax.ppermute(own, 'box', backward)  7.82 us
    ppermute x1, waiting for transfers between devices, on_device(): from_before = lax.ppermute(update[4:6], 'box', forward)  5.23 us
  transfers between devices with their start and end apart: 4, of which 2 were waited for; matrix products, arithmetic and copies ran while one was open for 1% of the time, Pallas kernels for 0%

profile of v1, /device:TPU:2, one launch (start us, length us, event | category | flops | bytes accessed | tf_op | source)
XLA Modules:
  0.0 161.3 jit_solution(2786054684914332359)
XLA Ops:
  0.6 0.0 copy-start.4
  0.6 0.7 convert_element_type.3
  1.3 0.0 copy-done.4
  1.4 0.0 copy-start.6
  1.4 0.0 copy-start.5
  1.4 0.0 copy-start.1
  1.4 7.8 %collective-permute-start.1 = (f32[2,4,512]{2,1,0:T(4,128)S(1)}, f32[2,4,512]{2,1,0:T(4,128)S(1)}, u32[]{:S(2)}, u32[]{:S(2)}) collective-permute-start(f32[2,4,512]{2,1,0:T(4,128)S(1)} %pad_maximum_fusion.own_ref), channel_id=1, source_target_pairs={{4,0},{8,4},{12,8},{16,12},{20,16},{24,20},{28,24},{32,28},{36,32}... | collective-permute-start | bytes 49160 | tf_op jit(solution)/shard_map/ppermute | solution.py:274
  9.2 0.0 collective-permute-start
  9.2 0.0 copy-done.6
  9.2 0.1 reshape.11
  9.3 0.0 copy-done.5
  9.3 12.5 %all-gather.1.shared_ref = f32[4,4,256]{2,1,0:T(4,128)} all-gather(f32[1,4,256]{2,1,0:T(4,128)S(1)} %maximum_bitcast_fusion), channel_id=2, replica_groups=mesh['box'=64,'col'=4] {'col'}, dimensions={0}, use_global_device_ids=true | all-gather | bytes 20480 | tf_op jit(solution)/shard_map/all_gather | solution.py:275
  21.8 0.0 copy-done.1
  21.8 0.0 collective-permute-done.1.after_ref
  21.8 0.0 copy-start.2
  21.8 0.0 collective-permute-done.before_ref
  21.8 0.6 copy-done.2
  22.4 0.0 copy-start.3
  22.4 0.6 copy-done.3
  23.0 124.8 %skeletonize.1 = (f32[2,2,256,64]{3,2,1,0:T(8,128)}, f32[6,128,256]{2,1,0:T(8,128)}) custom-call(s32[2,8]{1,0:T(2,128)} %boxes_ref.1, s32[2,8]{1,0:T(2,128)} %places_ref.1, f32[2,4,512]{2,1,0:T(4,128)} %copy-done.1, f32[2,4,512]{2,1,0:T(4,128)} %copy-done.3, f32[2,4,512]{2,1,0:T(4,128)} %copy-done.2, f32[4,4,256]{2,1,0:T(4,128)} %all-gather.1.shared_ref), custom_call_target="tpu_custom_call" | custom-call | tf_op jit(solution)/shard_map/skeletonize/pallas_call | solution.py:280
  147.8 0.0 copy-start
  147.8 1.2 fusion
  149.0 2.4 %collective-permute-start.3 = (f32[2,2,64,256]{3,2,1,0:T(8,128)S(1)}, f32[2,2,64,256]{3,2,1,0:T(8,128)S(1)}, u32[]{:S(2)}, u32[]{:S(2)}) collective-permute-start(f32[2,2,64,256]{3,2,1,0:T(8,128)S(1)} %bitcast.7), channel_id=1, source_target_pairs={{4,0},{8,4},{12,8},{16,12},{20,16},{24,20},{28,24},{32,28},{36,32}... | collective-permute-start | bytes 786440 | tf_op jit(solution)/shard_map/ppermute | solution.py:304
  151.5 0.0 collective-permute-start.2
  151.5 0.0 copy-done
  151.5 0.9 copy.11
  152.4 3.0 %collective-permute-done.3 = f32[2,2,64,256]{3,2,1,0:T(8,128)S(1)} collective-permute-done((f32[2,2,64,256]{3,2,1,0:T(8,128)S(1)}, f32[2,2,64,256]{3,2,1,0:T(8,128)S(1)}, u32[]{:S(2)}, u32[]{:S(2)}) %collective-permute-start.3) | collective-permute-done | bytes 262176 | tf_op jit(solution)/shard_map/ppermute | solution.py:304
  155.4 5.2 %collective-permute-done.2 = f32[2,2,64,256]{3,2,1,0:T(8,128)S(1)} collective-permute-done((f32[2,2,64,256]{3,2,1,0:T(8,128)S(1)}, f32[2,2,64,256]{3,2,1,0:T(8,128)S(1)}, u32[]{:S(2)}, u32[]{:S(2)}) %collective-permute-start.2) | collective-permute-done | bytes 262176 | tf_op jit(solution)/shard_map/ppermute | solution.py:303
  160.6 0.8 add_add_fusion
  (4 shorter events, 0.0 us)
Async XLA Ops:
  0.6 0.7 copy-start.4
  1.4 7.9 %copy-start.6 = (f32[2,2,64]{2,1,0:T(2,128)S(1)}, f32[2,2,64]{2,1,0:T(2,128)}, u32[]{:S(2)}) copy-start(f32[2,2,64]{2,1,0:T(2,128)} %param.11) | copy-start | bytes 3076
  1.4 8.0 %copy-start.5 = (f32[3,256]{1,0:T(4,128)S(1)}, f32[3,256]{1,0:T(4,128)}, u32[]{:S(2)}) copy-start(f32[3,256]{1,0:T(4,128)} %param.7) | copy-start | bytes 9220
  1.4 20.4 %copy-start.1 = (f32[2,4,512]{2,1,0:T(4,128)}, f32[2,4,512]{2,1,0:T(4,128)S(1)}, u32[]{:S(2)}) copy-start(f32[2,4,512]{2,1,0:T(4,128)S(1)} %pad_maximum_fusion.own_ref) | copy-start | bytes 49156
  1.4 20.4 %collective-permute-start.1 = (f32[2,4,512]{2,1,0:T(4,128)S(1)}, f32[2,4,512]{2,1,0:T(4,128)S(1)}, u32[]{:S(2)}, u32[]{:S(2)}) collective-permute-start(f32[2,4,512]{2,1,0:T(4,128)S(1)} %pad_maximum_fusion.own_ref), channel_id=1, source_target_pairs={{4,0},{8,4},{12,8},{16,12},{20,16},{24,20},{28,24},{32,28},{36,32}... | collective-permute-start | bytes 49160 | tf_op jit(solution)/shard_map/ppermute | solution.py:274
  9.2 12.6 %collective-permute-start = (f32[2,4,512]{2,1,0:T(4,128)S(1)}, f32[2,4,512]{2,1,0:T(4,128)S(1)}, u32[]{:S(2)}, u32[]{:S(2)}) collective-permute-start(f32[2,4,512]{2,1,0:T(4,128)S(1)} %pad_maximum_fusion.own_ref), channel_id=1, source_target_pairs={{0,4},{4,8},{8,12},{12,16},{16,20},{20,24},{24,28},{28,32},{32,36}... | collective-permute-start | bytes 49160 | tf_op jit(solution)/shard_map/ppermute | solution.py:273
  21.8 0.6 copy-start.2
  22.4 0.6 copy-start.3
  147.8 3.6 %copy-start = (f32[2,2,256,64]{3,2,1,0:T(8,128)S(1)}, f32[2,2,256,64]{3,2,1,0:T(8,128)}, u32[]{:S(2)}) copy-start(f32[2,2,256,64]{3,2,1,0:T(8,128)} %get-tuple-element.8) | copy-start | bytes 786436
  149.0 6.3 %collective-permute-start.3 = (f32[2,2,64,256]{3,2,1,0:T(8,128)S(1)}, f32[2,2,64,256]{3,2,1,0:T(8,128)S(1)}, u32[]{:S(2)}, u32[]{:S(2)}) collective-permute-start(f32[2,2,64,256]{3,2,1,0:T(8,128)S(1)} %bitcast.7), channel_id=1, source_target_pairs={{4,0},{8,4},{12,8},{16,12},{20,16},{24,20},{28,24},{32,28},{36,32}... | collective-permute-start | bytes 786440 | tf_op jit(solution)/shard_map/ppermute | solution.py:304
  151.5 9.1 %collective-permute-start.2 = (f32[2,2,64,256]{3,2,1,0:T(8,128)S(1)}, f32[2,2,64,256]{3,2,1,0:T(8,128)S(1)}, u32[]{:S(2)}, u32[]{:S(2)}) collective-permute-start(f32[2,2,64,256]{3,2,1,0:T(8,128)S(1)} %bitcast.6), channel_id=1, source_target_pairs={{0,4},{4,8},{8,12},{12,16},{16,20},{20,24},{24,28},{28,32},{32,36}... | collective-permute-start | bytes 786440 | tf_op jit(solution)/shard_map/ppermute | solution.py:303
